TPU v7x, 32 devices: a whole 2x2x4 slice. The times are simulated.
32 devices in a mesh: dp: 16 (over z, y, core), tensor: 2 (over x).
Axes of the slice: x: 2, y: 2, z: 4, core: 2. Of those that a mesh axis runs over, the one named last changes fastest.
Arguments:
- hidden_in: bfloat16 [8192, 768], P(('dp', 'tensor')), may hold values from -6 to 6
- attn_gain: float32 [768], replicated, may hold values from 0.5 to 1.5
- qkv_weight: bfloat16 [3, 768, 768], P(None, None, 'tensor'), may hold values from -0.21875 to 0.21875
- out_weight: bfloat16 [768, 768], P('tensor'), may hold values from -1.75 to 1.75
- mlp_gain: float32 [768], replicated, may hold values from 0.5 to 1.5
- in_weight: bfloat16 [2, 768, 1152], P(None, None, 'tensor'), may hold values from -0.21875 to 0.21875
- down_weight: bfloat16 [1152, 768], P('tensor'), may hold values from -0.1875 to 0.1875
- lengths: int32 [16, 4], P('dp'), may hold values from 0 to 512, as said below
- cotangent: bfloat16 [8192, 768], P(('dp', 'tensor')), may hold values from -6 to 6
Outputs:
- layer_out: bfloat16 [8192, 768], P(('dp', 'tensor'))
- grad_input: bfloat16 [8192, 768], P(('dp', 'tensor'))
- grad_attn_gain: float32 [768], replicated
- grad_qkv_weight: float32 [3, 768, 768], P(None, 'dp', 'tensor')
- grad_out_weight: float32 [768, 768], P('tensor', 'dp')
- grad_mlp_gain: float32 [768], replicated
- grad_in_weight: float32 [2, 768, 1152], P(None, 'dp', 'tensor')
- grad_down_weight: float32 [1152, 768], P('tensor', 'dp')
Inputs may be any that keep to these rules, and one draw needn't show every extreme that they name: In each row the lengths sum to more than 256 and at most 512; zero is an empty slot. The third sequence of each row begins before slot 256 and ends after it. In every draw one row is a single sequence of 512.
All inputs are finite; a program needn't handle non-finite values.
Results may differ from a plain program's by a relative error of at most 0.018.
Values may be sent and summed in bfloat16 or wider, within the bound.
A program may use at most 128 MiB of HBM per device.

v0:
```python
import jax
import jax.numpy as jnp
from jax import lax
from jax.sharding import PartitionSpec as P

HEAD_DIM = 64


EPSILON = 1e-05
ROPE_BASE = 160000.0


def positions(lengths_row, slot_count):
    token_index = jnp.arange(slot_count, dtype=jnp.int32)
    cumulative = jnp.cumsum(lengths_row)
    segment = jnp.sum((token_index[:, None] >= cumulative[None, :]).astype(jnp.int32), axis=1)
    bounds = jnp.concatenate([cumulative - lengths_row, cumulative[-1:]])
    pick_slot = segment[:, None] == jnp.arange(bounds.shape[0], dtype=jnp.int32)[None, :]
    doc_start = jnp.sum(jnp.where(pick_slot, bounds[None, :], 0), axis=1)
    return (segment, token_index - doc_start)


def rope_tables(position, head_width):
    half_dim = head_width // 2
    frequency = ROPE_BASE ** (-(2.0 * jnp.arange(half_dim, dtype=jnp.float32)) / head_width)
    angles = position.astype(jnp.float32)[:, None] * frequency[None, :]
    return (jnp.cos(angles), jnp.sin(angles))


def rotate(field, cosine, sine_table):
    half_dim = field.shape[-1] // 2
    first_half = field[..., :half_dim]
    second_half = field[..., half_dim:]
    cos_part = cosine[:, None, :]
    sin_part = sine_table[:, None, :]
    return jnp.concatenate(
        [
            first_half * cos_part - second_half * sin_part,
            second_half * cos_part + first_half * sin_part,
        ],
        axis=-1,
    )


def norm_parts(field, gain_vec):
    centred = field - jnp.mean(field, axis=-1, keepdims=True)
    variance = jnp.mean(centred * centred, axis=-1, keepdims=True)
    inv_std = lax.rsqrt(variance + EPSILON)
    standard = centred * inv_std
    return (standard * gain_vec, standard, inv_std)


def norm_back(gradient, gain_vec, standard, inv_std):
    scaled = gradient * gain_vec
    return inv_std * (
        scaled
        - jnp.mean(scaled, axis=-1, keepdims=True)
        - standard * jnp.mean(scaled * standard, axis=-1, keepdims=True)
    )


def gelu_exact(field):
    return jax.nn.gelu(field, approximate=False)


def on_device(
    hidden_in,
    attn_gain,
    qkv_weight,
    out_weight,
    mlp_gain,
    in_weight,
    down_weight,
    lengths,
    cotangent,
):
    tok_rows = hidden_in.shape[0]
    tok_group = tok_rows * lax.axis_size("tensor")
    local_width = qkv_weight.shape[2]
    head_shape = (tok_group, local_width // HEAD_DIM, HEAD_DIM)
    score_scale = HEAD_DIM ** (-0.5)
    segment, position = positions(lengths[0], tok_group)
    cosine, sine_table = rope_tables(position, HEAD_DIM)
    same_doc = (segment[:, None] == segment[None, :])[None]
    inputs_f = hidden_in.astype(jnp.float32)
    normed, standard_one, inv_one = norm_parts(inputs_f, attn_gain)
    normed_b = normed.astype(jnp.bfloat16)
    full_one = lax.all_gather(normed_b, "tensor", axis=0, tiled=True)
    qkv = jnp.einsum("td,cde->cte", full_one, qkv_weight, preferred_element_type=jnp.float32)
    queries = rotate(qkv[0].reshape(head_shape), cosine, sine_table).astype(jnp.bfloat16)
    key_rows = rotate(qkv[1].reshape(head_shape), cosine, sine_table).astype(jnp.bfloat16)
    value_rows = qkv[2].reshape(head_shape).astype(jnp.bfloat16)
    scores = (
        jnp.einsum("qhd,khd->hqk", queries, key_rows, preferred_element_type=jnp.float32)
        * score_scale
    )
    scores = jnp.where(same_doc, scores, -jnp.inf)
    row_peak = jnp.max(scores, axis=-1, keepdims=True)
    exponent = jnp.exp(scores - row_peak)
    row_total = jnp.sum(exponent, axis=-1, keepdims=True)
    logsum = row_peak + jnp.log(row_total)
    probs_b = (exponent / row_total).astype(jnp.bfloat16)
    attended = (
        jnp.einsum("hqk,khd->qhd", probs_b, value_rows, preferred_element_type=jnp.float32)
        .reshape(tok_group, local_width)
        .astype(jnp.bfloat16)
    )
    rows_in = attended
    branch = lax.psum_scatter(
        jnp.dot(rows_in, out_weight, preferred_element_type=jnp.float32).astype(jnp.bfloat16),
        "tensor",
        scatter_dimension=0,
        tiled=True,
    ).astype(jnp.float32)
    middle = inputs_f + branch
    normed_two, standard_two, inv_two = norm_parts(middle, mlp_gain)
    normed_two_b = normed_two.astype(jnp.bfloat16)
    full_two = lax.all_gather(normed_two_b, "tensor", axis=0, tiled=True)
    gate_up = jnp.einsum("td,cdf->ctf", full_two, in_weight, preferred_element_type=jnp.float32)
    active, gelu_pull = jax.vjp(gelu_exact, gate_up[0])
    hidden_b = (active * gate_up[1]).astype(jnp.bfloat16)
    rows_in = hidden_b
    branch_two = lax.psum_scatter(
        jnp.dot(rows_in, down_weight, preferred_element_type=jnp.float32).astype(jnp.bfloat16),
        "tensor",
        scatter_dimension=0,
        tiled=True,
    ).astype(jnp.float32)
    layer_out = (middle + branch_two).astype(jnp.bfloat16)
    grad_out = cotangent.astype(jnp.float32)
    grad_rows = lax.all_gather(cotangent, "tensor", axis=0, tiled=True)
    grad_down = lax.dot_general(
        hidden_b, grad_rows, (((0,), (0,)), ((), ())), preferred_element_type=jnp.float32
    )
    grad_hidden = lax.dot_general(
        grad_rows, down_weight, (((1,), (1,)), ((), ())), preferred_element_type=jnp.float32
    )
    grad_up = grad_hidden * active
    grad_gate = gelu_pull(grad_hidden * gate_up[1])[0]
    grad_gate_up = jnp.stack([grad_gate, grad_up]).astype(jnp.bfloat16)
    grad_in = jnp.einsum("td,ctf->cdf", full_two, grad_gate_up, preferred_element_type=jnp.float32)
    rows_in = grad_gate_up
    grad_normed_two = lax.psum_scatter(
        jnp.einsum("ctf,cdf->td", rows_in, in_weight, preferred_element_type=jnp.float32).astype(
            jnp.bfloat16
        ),
        "tensor",
        scatter_dimension=0,
        tiled=True,
    ).astype(jnp.float32)
    gain_two_part = jnp.sum(grad_normed_two * standard_two, axis=0)
    grad_middle = grad_out + norm_back(grad_normed_two, mlp_gain, standard_two, inv_two)
    grad_middle_b = grad_middle.astype(jnp.bfloat16)
    branch_grads = lax.all_gather(grad_middle_b, "tensor", axis=0, tiled=True)
    grad_wout = lax.dot_general(
        attended, branch_grads, (((0,), (0,)), ((), ())), preferred_element_type=jnp.float32
    )
    grad_attended = (
        lax.dot_general(
            branch_grads, out_weight, (((1,), (1,)), ((), ())), preferred_element_type=jnp.float32
        )
        .astype(jnp.bfloat16)
        .reshape(head_shape)
    )
    raw_scores = (
        jnp.einsum("qhd,khd->hqk", queries, key_rows, preferred_element_type=jnp.float32)
        * score_scale
    )
    attn_probs = jnp.where(same_doc, jnp.exp(raw_scores - logsum), 0.0)
    grad_probs = jnp.einsum(
        "qhd,khd->hqk", grad_attended, value_rows, preferred_element_type=jnp.float32
    )
    grad_values = jnp.einsum(
        "hqk,qhd->khd",
        attn_probs.astype(jnp.bfloat16),
        grad_attended,
        preferred_element_type=jnp.float32,
    )
    inner_sum = jnp.sum(attn_probs * grad_probs, axis=-1, keepdims=True)
    grad_scores = (attn_probs * (grad_probs - inner_sum)).astype(jnp.bfloat16)
    grad_queries = (
        jnp.einsum("hqk,khd->qhd", grad_scores, key_rows, preferred_element_type=jnp.float32)
        * score_scale
    )
    grad_keys = (
        jnp.einsum("hqk,qhd->khd", grad_scores, queries, preferred_element_type=jnp.float32)
        * score_scale
    )
    grad_qkv = jnp.stack(
        [
            rotate(grad_queries, cosine, -sine_table).reshape(tok_group, local_width),
            rotate(grad_keys, cosine, -sine_table).reshape(tok_group, local_width),
            grad_values.reshape(tok_group, local_width),
        ]
    ).astype(jnp.bfloat16)
    grad_wqkv = jnp.einsum("td,cte->cde", full_one, grad_qkv, preferred_element_type=jnp.float32)
    rows_in = grad_qkv
    grad_normed_one = lax.psum_scatter(
        jnp.einsum("cte,cde->td", rows_in, qkv_weight, preferred_element_type=jnp.float32).astype(
            jnp.bfloat16
        ),
        "tensor",
        scatter_dimension=0,
        tiled=True,
    ).astype(jnp.float32)
    gain_one_part = jnp.sum(grad_normed_one * standard_one, axis=0)
    grad_input = (
        grad_middle + norm_back(grad_normed_one, attn_gain, standard_one, inv_one)
    ).astype(jnp.bfloat16)
    gain_one, gain_two = lax.psum((gain_one_part, gain_two_part), ("dp", "tensor"))
    summed_qkv, summed_out, summed_in, summed_down = (
        lax.psum_scatter(grad_wqkv, "dp", scatter_dimension=1, tiled=True),
        lax.psum_scatter(grad_wout, "dp", scatter_dimension=1, tiled=True),
        lax.psum_scatter(grad_in, "dp", scatter_dimension=1, tiled=True),
        lax.psum_scatter(grad_down, "dp", scatter_dimension=1, tiled=True),
    )
    return (
        layer_out,
        grad_input,
        gain_one,
        summed_qkv,
        summed_out,
        gain_two,
        summed_in,
        summed_down,
    )


def solution(mesh):
    return jax.shard_map(
        on_device,
        mesh=mesh,
        in_specs=(
            P(("dp", "tensor"), None),
            P(),
            P(None, None, "tensor"),
            P("tensor", None),
            P(),
            P(None, None, "tensor"),
            P("tensor", None),
            P("dp", None),
            P(("dp", "tensor"), None),
        ),
        out_specs=(
            P(("dp", "tensor"), None),
            P(("dp", "tensor"), None),
            P(),
            P(None, "dp", "tensor"),
            P("tensor", "dp"),
            P(),
            P(None, "dp", "tensor"),
            P("tensor", "dp"),
        ),
        check_vma=False,
    )
```

profile of v0, /device:TPU:0, one launch (start us, length us, event | category | flops | bytes accessed | tf_op | source)
XLA Modules:
  0.0 492.0 jit_solution(18062828825736407155)
XLA Ops:
  11.1 12.7 %all_gather.12 = bf16[512,768]{1,0:T(8,128)(2,1)S(1)} all-gather(bf16[256,768]{1,0:T(8,128)(2,1)S(1)} %fusion.42), channel_id=1, replica_groups=mesh['dp'=16,'tensor'=2] {'tensor'}, dimensions={0}, use_global_device_ids=true | all-gather | bytes 1179648 | tf_op jit(solution)/shard_map/all_gather | solution.py:88
  38.6 14.4 %all_gather.14 = bf16[512,768]{1,0:T(8,128)(2,1)S(1)} all-gather(bf16[256,768]{1,0:T(8,128)(2,1)S(1)} %copy-done.8), channel_id=1, replica_groups=mesh['dp'=16,'tensor'=2] {'tensor'}, dimensions={0}, use_global_device_ids=true | all-gather | bytes 1179648 | tf_op jit(solution)/shard_map/all_gather | solution.py:131
  53.1 2.9 fusion.78
  55.9 3.2 reduce-scatter.7.cloned.1.call-done
  61.8 11.9 %all_gather.13 = bf16[512,768]{1,0:T(8,128)(2,1)S(1)} all-gather(bf16[256,768]{1,0:T(8,128)(2,1)S(1)} %multiply_convert_fusion.3), channel_id=1, replica_groups=mesh['dp'=16,'tensor'=2] {'tensor'}, dimensions={0}, use_global_device_ids=true | all-gather | bytes 1179648 | tf_op jit(solution)/shard_map/all_gather | solution.py:118
  75.4 2.8 fusion.61
  80.5 2.1 bitcast_convert_fusion.1
  83.5 17.9 %reduce-scatter.11.cloned.1.call-done = bf16[256,768]{1,0:T(8,128)(2,1)} async-done(((bf16[512,768]{1,0:T(8,128)(2,1)}), bf16[256,768]{1,0:T(8,128)(2,1)}) %reduce-scatter.11.cloned.1.call-update) | async-done | bytes 393232 | tf_op jit(solution)/shard_map/reduce_scatter | solution.py:143
  103.4 11.6 %all_gather.15 = bf16[512,768]{1,0:T(8,128)(2,1)S(1)} all-gather(bf16[256,768]{1,0:T(8,128)(2,1)S(1)} %fusion.75), channel_id=1, replica_groups=mesh['dp'=16,'tensor'=2] {'tensor'}, dimensions={0}, use_global_device_ids=true | all-gather | bytes 1179648 | tf_op jit(solution)/shard_map/all_gather | solution.py:154
  115.6 5.1 %fusion.8 = bf16[6,64,512]{2,1,0:T(8,128)(2,1)} fusion(bf16[512,6,64]{0,2,1:T(8,128)(2,1)S(1)} %bitcast.169, f32[6,512,512]{1,2,0:T(8,128)} %copy-done.2, f32[6,512]{1,0:T(8,128)S(1)} %log_add_fusion, pred[512,512]{0,1:T(8,128)(4,1)S(1)} %copy-done.7), kind=kOutput, calls=%fused_computation.24 | convolution fusion | flops 207814656 | bytes 7352320 | tf_op jit(solution)/shard_map/hqk,qhd->khd/dot_general | solution.py:173
  120.7 4.8 multiply_reduce_fusion
  125.5 4.7 multiply_convert_fusion
  138.3 4.0 bitcast_convert_fusion
  142.4 2.9 convolution_convert_fusion
  145.3 4.3 convolution_bitcast_fusion
  149.6 7.5 %copy.51 = f32[2,768,576]{2,0,1:T(2,128)} copy(f32[2,768,576]{1,2,0:T(8,128)} %convolution_bitcast_fusion) | data formatting | bytes 7077888 | tf_op jit(solution)/shard_map/td,ctf->cdf/transpose | solution.py:141
  157.1 4.5 convolution_bitcast_fusion.1
  161.6 6.2 %copy.50 = f32[3,768,384]{2,0,1:T(4,128)} copy(f32[3,768,384]{1,2,0:T(8,128)} %convolution_bitcast_fusion.1) | data formatting | bytes 7077888 | tf_op jit(solution)/shard_map/td,cte->cde/transpose | solution.py:196
  168.1 2.2 fusion.80
  176.3 40.6 %all-reduce.2 = (f32[768]{0:T(1024)}, f32[768]{0:T(1024)}) all-reduce(f32[768]{0:T(1024)S(1)} %get-tuple-element.34, f32[768]{0:T(1024)S(1)} %get-tuple-element.32), channel_id=1, replica_groups=mesh['dp'=16,'tensor'=2] {'dp','tensor'}, use_global_device_ids=true, to_apply=%region_19.20 | all-reduce | flops 1536 | bytes 12288 | tf_op jit(solution)/shard_map/psum | solution.py:210
  217.0 2.7 fusion.46
  219.8 137.8 %all-reduce.6.cloned.1.call-done = (f32[3,768,384]{2,0,1:T(4,128)}, f32[2,768,576]{2,0,1:T(2,128)}) async-done(((f32[3,768,384]{2,0,1:T(4,128)}, f32[2,768,576]{2,0,1:T(2,128)}), (f32[3,768,384]{2,0,1:T(4,128)}, f32[2,768,576]{2,0,1:T(2,128)})) %all-reduce.6.cloned.1.call-update) | async-done | bytes 7077904
  361.0 62.4 %reduce-scatter.17.cloned.1.call-done = f32[576,48]{0,1:T(8,128)} async-done(((f32[576,768]{0,1:T(8,128)}), f32[576,48]{0,1:T(8,128)}) %reduce-scatter.17.cloned.1.call-update) | async-done | bytes 110608 | tf_op jit(solution)/shard_map/reduce_scatter | solution.py:215
  423.4 61.7 %reduce-scatter.15.cloned.1.call-done = f32[384,48]{0,1:T(8,128)} async-done(((f32[384,768]{0,1:T(8,128)}), f32[384,48]{0,1:T(8,128)}) %reduce-scatter.15.cloned.1.call-update) | async-done | bytes 73744 | tf_op jit(solution)/shard_map/reduce_scatter | solution.py:213
  (167 shorter events, 45.4 us)
Async XLA Ops:
  7.2 66.6 %copy-start = (bf16[2,768,576]{1,2,0:T(8,128)(2,1)S(1)}, bf16[2,768,576]{1,2,0:T(8,128)(2,1)}, u32[]{:S(2)}) copy-start(bf16[2,768,576]{1,2,0:T(8,128)(2,1)} %param.14) | copy-start | bytes 5308420
  7.2 51.9 %reduce-scatter.7.cloned.1.call-start = ((), (), s32[]{:S(2)}) async-start(), calls=%async_computation.6 | async-start | bytes 1179648 | tf_op jit(solution)/shard_map/reduce_scatter | solution.py:109
  8.5 15.4 %copy-start.44 = (bf16[3,768,384]{2,1,0:T(8,128)(2,1)S(1)}, bf16[3,768,384]{2,1,0:T(8,128)(2,1)}, u32[]{:S(2)}) copy-start(bf16[3,768,384]{2,1,0:T(8,128)(2,1)} %param.11) | copy-start | bytes 5308420
  25.1 7.9 %copy-start.19 = (bf16[1,512,384]{1,2,0:T(8,128)(2,1)}, bf16[1,512,384]{1,2,0:T(8,128)(2,1)S(1)}, u32[]{:S(2)}) copy-start(bf16[1,512,384]{1,2,0:T(8,128)(2,1)S(1)} %slice.115) | copy-start | bytes 1179652
  27.2 5.8 %copy-start.6 = (pred[512,512]{0,1:T(8,128)(4,1)}, pred[512,512]{0,1:T(8,128)(4,1)S(1)}, u32[]{:S(2)}) copy-start(pred[512,512]{0,1:T(8,128)(4,1)S(1)} %broadcast_compare_fusion) | copy-start | bytes 786436
  38.6 62.8 %reduce-scatter.11.cloned.1.call-start = ((), (), s32[]{:S(2)}) async-start(), calls=%async_computation.8 | async-start | bytes 1179648 | tf_op jit(solution)/shard_map/reduce_scatter | solution.py:143
  53.1 6.1 %copy-start.3 = (bf16[256,768]{1,0:T(8,128)(2,1)S(1)}, bf16[256,768]{1,0:T(8,128)(2,1)}, u32[]{:S(2)}) copy-start(bf16[256,768]{1,0:T(8,128)(2,1)} %param.9) | copy-start | bytes 1179652
  55.9 5.7 %copy-start.34 = (f32[768]{0:T(1024)S(1)}, f32[768]{0:T(1024)}, u32[]{:S(2)}) copy-start(f32[768]{0:T(1024)} %param.13) | copy-start | bytes 9220
  82.6 20.4 %copy-start.9 = (bf16[256,768]{1,0:T(8,128)(2,1)S(1)}, bf16[256,768]{1,0:T(8,128)(2,1)}, u32[]{:S(2)}) copy-start(bf16[256,768]{1,0:T(8,128)(2,1)} %param.17) | copy-start | bytes 1179652
  82.6 92.2 %reduce-scatter.13.cloned.1.call-start = ((), (), s32[]{:S(2)}) async-start(), calls=%async_computation.9 | async-start | bytes 1179648 | tf_op jit(solution)/shard_map/reduce_scatter | solution.py:198
  103.0 12.1 %copy-start.40 = (f32[256]{0:T(256)}, f32[256]{0:T(256)S(1)}, u32[]{:S(2)}) copy-start(f32[256]{0:T(256)S(1)} %get-tuple-element.69) | copy-start | bytes 3076
  103.0 12.1 %copy-start.42 = (f32[256]{0:T(256)}, f32[256]{0:T(256)S(1)}, u32[]{:S(2)}) copy-start(f32[256]{0:T(256)S(1)} %get-tuple-element.70) | copy-start | bytes 3076
  103.0 12.1 %copy-start.29 = (bf16[384,768]{1,0:T(8,128)(2,1)S(1)}, bf16[384,768]{1,0:T(8,128)(2,1)}, u32[]{:S(2)}) copy-start(bf16[384,768]{1,0:T(8,128)(2,1)} %param.12) | copy-start | bytes 1769476
  103.0 12.6 %copy-start.7 = (pred[512,512]{0,1:T(8,128)(4,1)S(1)}, pred[512,512]{0,1:T(8,128)(4,1)}, u32[]{:S(2)}) copy-start(pred[512,512]{0,1:T(8,128)(4,1)} %copy-done.6) | copy-start | bytes 786436
  103.4 17.3 %slice-start = ((s8[6291456]{0:T(1024)(128)(4,1)}), s8[4194304]{0:T(1024)(128)(4,1)S(1)}, s32[]{:S(2)}) async-start(s8[6291456]{0:T(1024)(128)(4,1)} %bitcast.158), calls=%async_computation.13 | async-start | bytes 8388608
  142.3 74.7 %reduce-scatter.9.cloned.1.call-start = ((), (), s32[]{:S(2)}) async-start(), calls=%async_computation.7 | async-start | bytes 1179648 | tf_op jit(solution)/shard_map/reduce_scatter | solution.py:123
  145.2 212.3 %all-reduce.6.cloned.1.call-start = ((), (), s32[]{:S(2)}) async-start(), calls=%async_computation.12 | async-start | bytes 17301504
  167.8 255.6 %reduce-scatter.17.cloned.1.call-start = ((), (), s32[]{:S(2)}) async-start(), calls=%async_computation.11 | async-start | bytes 2088960 | tf_op jit(solution)/shard_map/reduce_scatter | solution.py:215
  170.3 314.8 %reduce-scatter.15.cloned.1.call-start = ((), (), s32[]{:S(2)}) async-start(), calls=%async_computation.10 | async-start | bytes 1253376 | tf_op jit(solution)/shard_map/reduce_scatter | solution.py:213
  172.9 44.1 %copy-start.10 = (bf16[256,768]{1,0:T(8,128)(2,1)S(1)}, bf16[256,768]{1,0:T(8,128)(2,1)}, u32[]{:S(2)}) copy-start(bf16[256,768]{1,0:T(8,128)(2,1)} %param.17) | copy-start | bytes 1179652
  172.9 44.1 %copy-start.12 = (bf16[256,768]{1,0:T(8,128)(2,1)S(1)}, bf16[256,768]{1,0:T(8,128)(2,1)}, u32[]{:S(2)}) copy-start(bf16[256,768]{1,0:T(8,128)(2,1)} %reduce-scatter.11.cloned.1.call-done) | copy-start | bytes 1179652
  172.9 44.1 %copy-start.41 = (f32[256]{0:T(256)S(1)}, f32[256]{0:T(256)}, u32[]{:S(2)}) copy-start(f32[256]{0:T(256)} %copy-done.40) | copy-start | bytes 3076
  172.9 44.1 %copy-start.43 = (f32[256]{0:T(256)S(1)}, f32[256]{0:T(256)}, u32[]{:S(2)}) copy-start(f32[256]{0:T(256)} %copy-done.42) | copy-start | bytes 3076
  217.0 268.1 %copy-start.1 = (bf16[2,768,576]{1,2,0:T(8,128)(2,1)S(1)}, bf16[2,768,576]{1,2,0:T(8,128)(2,1)}, u32[]{:S(2)}) copy-start(bf16[2,768,576]{1,2,0:T(8,128)(2,1)} %param.14) | copy-start | bytes 5308420
  (32 other events, 69.9 us)
Sparse Core Ops, SparseCore 0:
  38.7 20.3 reduce-scatter.6
  82.8 18.6 reduce-scatter.10
  142.4 17.4 reduce-scatter.12
  162.1 17.4 reduce-scatter.8
  183.1 174.4 all-reduce.5
  362.2 61.1 reduce-scatter.16
  428.0 57.0 reduce-scatter.14
where the time goes:
time: 493 us; the launch traced here: 492 us
  waiting for transfers between devices  283 us (57%)
  blocking collectives  91.4 us (19%)
  matrix products  45.3 us (9%)
  other arithmetic  29.1 us (6%)
  local copies, waits for them, and re-layouts  27.1 us (5%)
  between operations  15.4 us (3%)
    unnamed x8, waiting for transfers between devices  138 us
    reduce_scatter x1, waiting for transfers between devices, on_device(): lax.psum_scatter(grad_down, 'dp', scatter_dimension=1, tiled=True)  62.4 us
    reduce_scatter x1, waiting for transfers between devices, on_device(): lax.psum_scatter(grad_wout, 'dp', scatter_dimension=1, tiled=True)  61.7 us
    psum x1, blocking collectives, on_device(): lax.psum((gain_one_part, gain_two_part), ('dp', 'tensor'))  40.6 us
    reduce_scatter x1, waiting for transfers between devices, on_device(): lax.psum_scatter(jnp.einsum('ctf,cdf->td', rows_in, in_weight, preferred_...  17.9 us
    all_gather x1, blocking collectives, on_device(): grad_rows = lax.all_gather(cotangent, 'tensor', axis=0, tiled=True)  14.4 us
    all_gather x1, blocking collectives, on_device(): full_one = lax.all_gather(normed_b, 'tensor', axis=0, tiled=True)  12.7 us
    all_gather x1, blocking collectives, on_device(): full_two = lax.all_gather(normed_two_b, 'tensor', axis=0, tiled=True)  11.9 us
  transfers between devices with their start and end apart: 7, of which 5 were waited for; matrix products, arithmetic and copies ran while one was open for 8% of the time, Pallas kernels for 0%

commit v1 on v0

--- a/solution.py
+++ b/solution.py
@@ -1,6 +1,10 @@
+import functools
+
 import jax
 import jax.numpy as jnp
 from jax import lax
+from jax.experimental import pallas as pl
+from jax.experimental.pallas import tpu as pltpu
 from jax.sharding import PartitionSpec as P
 
 HEAD_DIM = 64
@@ -61,6 +65,140 @@
 
 def gelu_exact(field):
     return jax.nn.gelu(field, approximate=False)
+
+
+def partner_of(place, bit):
+    side = (place // (1 << bit)) % 2
+    return place + (1 - 2 * side) * (1 << bit), side
+
+
+def halving_kernel(bits, count, *refs):
+    parts, gains = refs[:count], refs[count]
+    outs, gains_out = refs[count + 1 : 2 * count + 1], refs[2 * count + 1]
+    scratch = refs[2 * count + 2 :]
+    landed = [scratch[c * bits : (c + 1) * bits] for c in range(count)]
+    gain_land, gain_sum, send_sem, recv_sem, gain_send, gain_recv = scratch[count * bits :]
+    me = lax.axis_index("dp")
+    across = 1 - lax.axis_index("tensor")
+    pairs = [partner_of(me, b) for b in range(bits)]
+    targets = [{"dp": p} for p, _ in pairs] + [{"tensor": across}]
+
+    barrier = pltpu.get_barrier_semaphore()
+    for target in targets:
+        pl.semaphore_signal(barrier, inc=1, device_id=target, device_id_type=pl.DeviceIdType.MESH)
+    pl.semaphore_wait(barrier, bits + 1)
+
+    def held(c, step):
+        return parts[c] if step == 0 else landed[c][step - 1]
+
+    def copy_of(c, step):
+        lead = (slice(None),) * (bits - step - 1)
+        return pltpu.make_async_remote_copy(
+            src_ref=held(c, step).at[lead + (1 - pairs[step][1],)],
+            dst_ref=landed[c][step],
+            send_sem=send_sem.at[c, step],
+            recv_sem=recv_sem.at[c, step],
+            device_id=targets[step],
+            device_id_type=pl.DeviceIdType.MESH,
+        )
+
+    def gain_copy(step):
+        return pltpu.make_async_remote_copy(
+            src_ref=gains if step == 0 else gain_sum.at[step - 1],
+            dst_ref=gain_land.at[step],
+            send_sem=gain_send.at[step],
+            recv_sem=gain_recv.at[step],
+            device_id=targets[step],
+            device_id_type=pl.DeviceIdType.MESH,
+        )
+
+    def finish(c, step):
+        copy_of(c, step).wait_recv()
+        side = pairs[step][1]
+        dims = bits - step - 1
+        last = step == bits - 1
+
+        def add(i, _):
+            at = tuple((i // (1 << (dims - 1 - d))) % 2 for d in range(dims))
+            total = landed[c][step][at].astype(jnp.float32) + held(c, step)[at + (side,)].astype(
+                jnp.float32
+            )
+            if last:
+                outs[c][...] = total
+            else:
+                landed[c][step][at] = total.astype(jnp.bfloat16)
+            return 0
+
+        if last:
+            add(0, 0)
+        else:
+            lax.fori_loop(0, 1 << dims, add, 0)
+
+    def finish_gain(step):
+        gain_copy(step).wait_recv()
+        before = gains[...] if step == 0 else gain_sum[step - 1]
+        if step == bits:
+            gains_out[...] = before + gain_land[step]
+        else:
+            gain_sum[step] = before + gain_land[step]
+
+    for tick in range(max(count, 2) + bits):
+        for step in range(bits, -1, -1):
+            c = tick - step
+            if 0 <= c < count:
+                if step > 0:
+                    finish(c, step - 1)
+                if step < bits:
+                    copy_of(c, step).start()
+        if 0 < tick <= bits + 1:
+            finish_gain(tick - 1)
+        if tick <= bits:
+            gain_copy(tick).start()
+    for c in range(count):
+        for step in range(bits):
+            copy_of(c, step).wait_send()
+    for step in range(bits + 1):
+        gain_copy(step).wait_send()
+
+
+def reduce_over_groups(grads, gains):
+    groups = lax.axis_size("dp")
+    bits = groups.bit_length() - 1
+    rows = grads[0].shape[0] // groups
+    padded = -(-rows // 16) * 16
+    blocks = []
+    for grad in grads:
+        block = grad.astype(jnp.bfloat16).reshape(groups, rows, grad.shape[1])
+        if padded != rows:
+            block = jnp.pad(block, ((0, 0), (0, padded - rows), (0, 0)))
+        blocks.append(block.reshape((2,) * bits + (padded, grad.shape[1])))
+    count = len(grads)
+    vmem = pl.BlockSpec(memory_space=pltpu.VMEM)
+    scratch = [
+        pltpu.VMEM((2,) * (bits - step - 1) + (padded, grad.shape[1]), jnp.bfloat16)
+        for grad in grads
+        for step in range(bits)
+    ]
+    results = pl.pallas_call(
+        functools.partial(halving_kernel, bits, count),
+        out_shape=[jax.ShapeDtypeStruct((padded, g.shape[1]), jnp.float32) for g in grads]
+        + [jax.ShapeDtypeStruct(gains.shape, jnp.float32)],
+        in_specs=[vmem] * (count + 1),
+        out_specs=[vmem] * (count + 1),
+        scratch_shapes=scratch
+        + [
+            pltpu.VMEM((bits + 1,) + gains.shape, jnp.float32),
+            pltpu.VMEM((bits,) + gains.shape, jnp.float32),
+            pltpu.SemaphoreType.DMA((count, bits)),
+            pltpu.SemaphoreType.DMA((count, bits)),
+            pltpu.SemaphoreType.DMA((bits + 1,)),
+            pltpu.SemaphoreType.DMA((bits + 1,)),
+        ],
+        compiler_params=pltpu.CompilerParams(
+            collective_id=0, has_side_effects=True, vmem_limit_bytes=48 * 1024 * 1024
+        ),
+    )(*blocks, gains)
+    return [r[:rows] for r in results[:count]], results[count]
 
 
 def on_device(
@@ -130,7 +268,7 @@
     grad_out = cotangent.astype(jnp.float32)
     grad_rows = lax.all_gather(cotangent, "tensor", axis=0, tiled=True)
     grad_down = lax.dot_general(
-        hidden_b, grad_rows, (((0,), (0,)), ((), ())), preferred_element_type=jnp.float32
+        grad_rows, hidden_b, (((0,), (0,)), ((), ())), preferred_element_type=jnp.float32
     )
     grad_hidden = lax.dot_general(
         grad_rows, down_weight, (((1,), (1,)), ((), ())), preferred_element_type=jnp.float32
@@ -153,7 +291,7 @@
     grad_middle_b = grad_middle.astype(jnp.bfloat16)
     branch_grads = lax.all_gather(grad_middle_b, "tensor", axis=0, tiled=True)
     grad_wout = lax.dot_general(
-        attended, branch_grads, (((0,), (0,)), ((), ())), preferred_element_type=jnp.float32
+        branch_grads, attended, (((0,), (0,)), ((), ())), preferred_element_type=jnp.float32
     )
     grad_attended = (
         lax.dot_general(
@@ -207,13 +345,17 @@
     grad_input = (
         grad_middle + norm_back(grad_normed_one, attn_gain, standard_one, inv_one)
     ).astype(jnp.bfloat16)
-    gain_one, gain_two = lax.psum((gain_one_part, gain_two_part), ("dp", "tensor"))
-    summed_qkv, summed_out, summed_in, summed_down = (
-        lax.psum_scatter(grad_wqkv, "dp", scatter_dimension=1, tiled=True),
-        lax.psum_scatter(grad_wout, "dp", scatter_dimension=1, tiled=True),
-        lax.psum_scatter(grad_in, "dp", scatter_dimension=1, tiled=True),
-        lax.psum_scatter(grad_down, "dp", scatter_dimension=1, tiled=True),
-    )
+    gains = jnp.concatenate(
+        [gain_one_part[None], gain_two_part[None], jnp.zeros((6, gain_one_part.shape[0]), jnp.float32)]
+    )
+    sums, gains = reduce_over_groups(
+        [grad_in[0], grad_in[1], grad_down, grad_wout, grad_wqkv[0], grad_wqkv[1], grad_wqkv[2]], gains
+    )
+    gain_one, gain_two = gains[0], gains[1]
+    summed_in = jnp.stack(sums[:2])
+    summed_down = sums[2].T
+    summed_out = sums[3].T
+    summed_qkv = jnp.stack(sums[4:])
     return (
         layer_out,
         grad_input,

time: 493 us -> 240 us (0.49)
  waiting for transfers between devices: 283 us -> 21 us
  Pallas kernels: 0 us -> 52 us
  blocking collectives: 91.4 us -> 51 us
    unnamed x8 -> x4, waiting for transfers between devices: 138 us -> 0.07 us
    reduce_scatter x2 -> x0, waiting for transfers between devices: 124 us -> none  [the longest x1 62.4 us: on_device(): lax.psum_scatter(grad_down, 'dp', scatter_dimension=1, tiled=True)]
    pallas_call x0 -> x1, Pallas kernels: none -> 52 us  [reduce_over_groups(): pl.pallas_call(functools.partial(halving_kernel, bits, count), out_shape=...]
    psum x1 -> x0, blocking collectives: 40.6 us -> none  [on_device(): lax.psum((gain_one_part, gain_two_part), ('dp', 'tensor'))]
    transpose x2 -> x0, local copies, waits for them, and re-layouts: 13.7 us -> none  [the longest x1 7.48 us: on_device(): jnp.einsum('td,ctf->cdf', full_two, grad_gate_up, preferred_element_type=...]
    slice x0 -> x8, local copies, waits for them, and re-layouts: none -> 12.9 us  [the longest x2 3.58 us: on_device(): grad_in[1]]
    unnamed x103 -> x106, local copies, waits for them, and re-layouts: 8.97 us -> 11.2 us
  transfers between devices with their start and end apart: 7 -> 4, of which waited for: 5 -> 2; matrix products, arithmetic and copies ran while one was open for 8% -> 14% of each run, Pallas kernels for 0% -> 22%
where the time goes in v1:
time: 240 us; the launch traced here: 239 us
  Pallas kernels  52 us (22%)
  blocking collectives  51 us (21%)
  matrix products  40.5 us (17%)
  local copies, waits for them, and re-layouts  31.4 us (13%)
  other arithmetic  28.6 us (12%)
  waiting for transfers between devices  21 us (9%)
  between operations  14.4 us (6%)
    pallas_call x1, Pallas kernels, reduce_over_groups(): pl.pallas_call(functools.partial(halving_kernel, bits, count), out_shape=...  52 us
    reduce_scatter x1, waiting for transfers between devices, on_device(): lax.psum_scatter(jnp.einsum('ctf,cdf->td', rows_in, in_weight, preferred_...  18.7 us
    all_gather x1, blocking collectives, on_device(): grad_rows = lax.all_gather(cotangent, 'tensor', axis=0, tiled=True)  14.4 us
    all_gather x1, blocking collectives, on_device(): full_one = lax.all_gather(normed_b, 'tensor', axis=0, tiled=True)  12.7 us
    all_gather x1, blocking collectives, on_device(): full_two = lax.all_gather(normed_two_b, 'tensor', axis=0, tiled=True)  11.9 us
    all_gather x1, blocking collectives, on_device(): branch_grads = lax.all_gather(grad_middle_b, 'tensor', axis=0, tiled=True)  11.9 us
    unnamed x106, local copies, waits for them, and re-layouts  11.2 us
    dot_general x1, matrix products, on_device(): jnp.einsum('hqk,qhd->khd', attn_probs.astype(jnp.bfloat16), grad_attended...  5.07 us
  transfers between devices with their start and end apart: 4, of which 2 were waited for; matrix products, arithmetic and copies ran while one was open for 14% of the time, Pallas kernels for 22%

profile of v1, /device:TPU:0, one launch (start us, length us, event | category | flops | bytes accessed | tf_op | source)
XLA Modules:
  0.0 239.2 jit_solution(13529021795598608051)
XLA Ops:
  13.2 12.7 %all_gather.12 = bf16[512,768]{1,0:T(8,128)(2,1)S(1)} all-gather(bf16[256,768]{1,0:T(8,128)(2,1)S(1)} %fusion.43), channel_id=1, replica_groups=mesh['dp'=16,'tensor'=2] {'tensor'}, dimensions={0}, use_global_device_ids=true | all-gather | bytes 1179648 | tf_op jit(solution)/shard_map/all_gather | solution.py:226
  37.8 14.4 %all_gather.14 = bf16[512,768]{1,0:T(8,128)(2,1)S(1)} all-gather(bf16[256,768]{1,0:T(8,128)(2,1)S(1)} %copy-done.12), channel_id=1, replica_groups=mesh['dp'=16,'tensor'=2] {'tensor'}, dimensions={0}, use_global_device_ids=true | all-gather | bytes 1179648 | tf_op jit(solution)/shard_map/all_gather | solution.py:269
  53.2 2.9 %fusion.81 = f32[512,576]{0,1:T(8,128)} fusion(bf16[512,768]{1,0:T(8,128)(2,1)S(1)} %all_gather.14, bf16[576,768]{1,0:T(8,128)(2,1)} %param.15), kind=kOutput, calls=%fused_computation.159 | convolution fusion | flops 452984832 | bytes 2850816 | tf_op jit(solution)/shard_map/dot_general | solution.py:273
  56.1 2.2 reduce-scatter.5.cloned.1.call-done
  61.0 11.9 %all_gather.13 = bf16[512,768]{1,0:T(8,128)(2,1)S(1)} all-gather(bf16[256,768]{1,0:T(8,128)(2,1)S(1)} %multiply_convert_fusion.3), channel_id=1, replica_groups=mesh['dp'=16,'tensor'=2] {'tensor'}, dimensions={0}, use_global_device_ids=true | all-gather | bytes 1179648 | tf_op jit(solution)/shard_map/all_gather | solution.py:256
  74.6 2.8 %fusion.62 = (bf16[1,512,576]{1,2,0:T(8,128)(2,1)S(1)}, f32[512,576]{0,1:T(8,128)S(1)}) fusion(f32[512,576]{0,1:T(8,128)S(1)} %copy-done.11, f32[2,512,576]{1,2,0:T(8,128)S(1)} %convolution_bitcast_fusion), kind=kLoop, calls=%fused_computation.104 | loop fusion | flops 21528576 | bytes 5308416 | tf_op jit(solution)/shard_map/stack | solution.py:278
  79.7 2.2 bitcast_convert_fusion.1
  81.9 18.7 %reduce-scatter.9.cloned.1.call-done = bf16[256,768]{1,0:T(8,128)(2,1)} async-done(((bf16[512,768]{1,0:T(8,128)(2,1)}), bf16[256,768]{1,0:T(8,128)(2,1)}) %reduce-scatter.9.cloned.1.call-update) | async-done | bytes 393232 | tf_op jit(solution)/shard_map/reduce_scatter | solution.py:281
  100.6 2.1 fusion.53
  103.2 11.9 %all_gather.15 = bf16[512,768]{1,0:T(8,128)(2,1)S(1)} all-gather(bf16[256,768]{1,0:T(8,128)(2,1)S(1)} %fusion.76), channel_id=1, replica_groups=mesh['dp'=16,'tensor'=2] {'tensor'}, dimensions={0}, use_global_device_ids=true | all-gather | bytes 1179648 | tf_op jit(solution)/shard_map/all_gather | solution.py:292
  116.5 5.1 %fusion.9 = bf16[6,64,512]{2,1,0:T(8,128)(2,1)} fusion(bf16[512,6,64]{0,2,1:T(8,128)(2,1)S(1)} %bitcast.198, f32[6,512,512]{1,2,0:T(8,128)} %copy-done.6, f32[6,512]{1,0:T(8,128)S(1)} %log_add_fusion, pred[512,512]{0,1:T(8,128)(4,1)S(1)} %broadcast_compare_fusion), kind=kOutput, calls=%fused_computation.27 | convolution fusion | flops 207814656 | bytes 7352320 | tf_op jit(solution)/shard_map/hqk,qhd->khd/dot_general | solution.py:311
  121.6 3.0 %multiply_reduce_fusion = (f32[6,512]{1,0:T(8,128)}, f32[6,512,512]{1,2,0:T(8,128)S(1)}) fusion(f32[6,512,512]{1,2,0:T(8,128)S(1)} %bitcast.188, f32[6,512]{1,0:T(8,128)S(1)} %log_add_fusion, pred[512,512]{0,1:T(8,128)(4,1)S(1)} %broadcast_compare_fusion, bf16[512,6,64]{0,2,1:T(8,128)(2,1)S(1)} %bitcast.199, bf16[512,6,64]{0,2,1:T(8,128)(2,1)S(1)} %bitcast.196), kind=kOutput, calls=%fused_computation.1 | convolution fusion | flops 209187840 | bytes 13656064 | tf_op jit(solution)/shard_map/qhd,khd->hqk/dot_general | solution.py:308
  124.5 2.7 %multiply_convert_fusion = bf16[6,512,512]{1,2,0:T(8,128)(2,1)S(1)} fusion(f32[6,512,512]{1,2,0:T(8,128)S(1)} %get-tuple-element.63, f32[6,512,512]{1,2,0:T(8,128)S(1)} %bitcast.188, f32[6,512]{1,0:T(8,128)} %get-tuple-element.62, f32[6,512]{1,0:T(8,128)} %copy-done.38, pred[512,512]{0,1:T(8,128)(4,1)S(1)} %broadcast_compare_fusion), kind=kLoop, calls=%fused_computation | loop fusion | flops 9437184 | bytes 16015360 | tf_op jit(solution)/shard_map/convert_element_type | solution.py:318
  127.2 3.0 %fusion.7 = f32[512,6,64]{0,2,1:T(8,128)} fusion(bf16[6,512,512]{1,2,0:T(8,128)(2,1)S(1)} %multiply_convert_fusion, bf16[512,6,32]{0,2,1:T(8,128)(2,1)} %copy-done.26, bf16[512,6,32]{0,2,1:T(8,128)(2,1)} %copy-done.25), kind=kOutput, calls=%fused_computation.24 | convolution fusion | flops 202309632 | bytes 4325376 | tf_op jit(solution)/shard_map/hqk,qhd->khd/dot_general | solution.py:324
  137.1 3.9 %bitcast_convert_fusion = bf16[512,768]{1,0:T(8,128)(2,1)} fusion(bf16[3,768,384]{2,1,0:T(8,128)(2,1)} %param.11, bf16[1,512,384]{2,1,0:T(8,128)(2,1)S(1)} %copy-done.36, bf16[1,512,384]{2,1,0:T(8,128)(2,1)} %copy.38, bf16[1,512,384]{2,1,0:T(8,128)(2,1)} %copy.37), kind=kOutput, calls=%fused_computation.16 | convolution fusion | flops 907542528 | bytes 3735552 | tf_op jit(solution)/shard_map/cte,cde->td/dot_general | solution.py:337
  145.2 2.3 convert_bitcast_fusion.1
  148.9 2.2 copy.41
  151.1 2.2 copy.40
  153.3 3.1 %convolution_convert_fusion.1 = bf16[512,768]{1,0:T(8,128)(2,1)} fusion(bf16[512,576]{0,1:T(8,128)(2,1)} %get-tuple-element.35, bf16[576,768]{1,0:T(8,128)(2,1)} %param.15), kind=kOutput, calls=%fused_computation.19 | convolution fusion | flops 453378048 | bytes 2260992 | tf_op jit(solution)/shard_map/dot_general | solution.py:262
  156.5 2.4 convert_bitcast_fusion
  160.6 2.1 copy.46
  162.7 2.1 copy.45
  174.4 52.0 %shard_map.152 = (f32[48,576]{1,0:T(8,128)S(1)}, f32[48,576]{1,0:T(8,128)S(1)}, f32[48,576]{1,0:T(8,128)S(1)}, f32[48,384]{1,0:T(8,128)S(1)}, f32[48,384]{1,0:T(...) custom-call(bf16[2,2,2,2,48,576]{5,4,3,2,1,0:T(8,128)(2,1)S(1)} %bitcast.175, ...), custom_call_target="tpu_custom_call" | custom-call | tf_op jit(solution)/shard_map/pallas_call | solution.py:182
  228.5 2.9 %fusion.47 = (bf16[256,768]{1,0:T(8,128)(2,1)}, bf16[256,768]{1,0:T(8,128)(2,1)}) fusion(bf16[256,768]{1,0:T(8,128)(2,1)S(1)} %copy-done.8, bf16[256,768]{1,0:T(8,128)(2,1)} %reduce-scatter.11.cloned.1.call-done, f32[256]{0:T(256)S(1)} %broadcast_multiply_fusion, f32[256]{0:T(256)S(1)} %broadcast_multiply_fusion.1, f32[768]{0:T(1024)S(1)} %copy-done.40, ...), kind=kLoop, calls=%fused_computation.84 | loop fusion | flops 5111808 | bytes 3160064 | tf_op jit(solution)/shard_map/convert_element_type | solution.py:347
  (175 shorter events, 53.8 us)
Async XLA Ops:
  7.2 65.8 %copy-start = (bf16[2,768,576]{1,2,0:T(8,128)(2,1)S(1)}, bf16[2,768,576]{1,2,0:T(8,128)(2,1)}, u32[]{:S(2)}) copy-start(bf16[2,768,576]{1,2,0:T(8,128)(2,1)} %param.14) | copy-start | bytes 5308420
  7.2 51.1 %reduce-scatter.5.cloned.1.call-start = ((), (), s32[]{:S(2)}) async-start(), calls=%async_computation.4 | async-start | bytes 1179648 | tf_op jit(solution)/shard_map/reduce_scatter | solution.py:247
  10.6 15.4 %copy-start.49 = (bf16[3,768,384]{2,1,0:T(8,128)(2,1)S(1)}, bf16[3,768,384]{2,1,0:T(8,128)(2,1)}, u32[]{:S(2)}) copy-start(bf16[3,768,384]{2,1,0:T(8,128)(2,1)} %param.11) | copy-start | bytes 5308420
  27.1 5.1 %copy-start.19 = (bf16[1,512,384]{1,2,0:T(8,128)(2,1)}, bf16[1,512,384]{1,2,0:T(8,128)(2,1)S(1)}, u32[]{:S(2)}) copy-start(bf16[1,512,384]{1,2,0:T(8,128)(2,1)S(1)} %slice.155) | copy-start | bytes 1179652
  37.8 62.8 %reduce-scatter.9.cloned.1.call-start = ((), (), s32[]{:S(2)}) async-start(), calls=%async_computation.6 | async-start | bytes 1179648 | tf_op jit(solution)/shard_map/reduce_scatter | solution.py:281
  53.2 5.1 %copy-start.7 = (bf16[256,768]{1,0:T(8,128)(2,1)S(1)}, bf16[256,768]{1,0:T(8,128)(2,1)}, u32[]{:S(2)}) copy-start(bf16[256,768]{1,0:T(8,128)(2,1)} %param.9) | copy-start | bytes 1179652
  56.1 4.7 %copy-start.39 = (f32[768]{0:T(1024)S(1)}, f32[768]{0:T(1024)}, u32[]{:S(2)}) copy-start(f32[768]{0:T(1024)} %param.13) | copy-start | bytes 9220
  60.8 41.9 %copy-start.41 = (f32[256]{0:T(256)}, f32[256]{0:T(256)S(1)}, u32[]{:S(2)}) copy-start(f32[256]{0:T(256)S(1)} %add_rsqrt_fusion) | copy-start | bytes 3076
  81.8 86.2 %reduce-scatter.11.cloned.1.call-start = ((), (), s32[]{:S(2)}) async-start(), calls=%async_computation.7 | async-start | bytes 1179648 | tf_op jit(solution)/shard_map/reduce_scatter | solution.py:336
  81.9 39.7 %copy-start.38 = (f32[6,512]{1,0:T(8,128)}, f32[6,512]{1,0:T(8,128)S(1)}, u32[]{:S(2)}) copy-start(f32[6,512]{1,0:T(8,128)S(1)} %log_add_fusion) | copy-start | bytes 36868
  102.7 12.3 %copy-start.46 = (f32[256]{0:T(256)}, f32[256]{0:T(256)S(1)}, u32[]{:S(2)}) copy-start(f32[256]{0:T(256)S(1)} %get-tuple-element.64) | copy-start | bytes 3076
  102.7 12.3 %copy-start.47 = (f32[256]{0:T(256)}, f32[256]{0:T(256)S(1)}, u32[]{:S(2)}) copy-start(f32[256]{0:T(256)S(1)} %get-tuple-element.65) | copy-start | bytes 3076
  102.8 13.2 %copy-start.34 = (bf16[384,768]{1,0:T(8,128)(2,1)S(1)}, bf16[384,768]{1,0:T(8,128)(2,1)}, u32[]{:S(2)}) copy-start(bf16[384,768]{1,0:T(8,128)(2,1)} %param.12) | copy-start | bytes 1769476
  103.2 18.4 %slice-start = ((s8[6291456]{0:T(1024)(128)(4,1)}), s8[4194304]{0:T(1024)(128)(4,1)S(1)}, s32[]{:S(2)}) async-start(s8[6291456]{0:T(1024)(128)(4,1)} %bitcast.187), calls=%async_computation.8 | async-start | bytes 8388608
  116.5 5.1 %slice-start.1 = ((s8[6291456]{0:T(1024)(128)(4,1)}), s8[2097152]{0:T(1024)(128)(4,1)S(1)}, s32[]{:S(2)}) async-start(s8[6291456]{0:T(1024)(128)(4,1)} %bitcast.187), calls=%async_computation.9 | async-start | bytes 4194304
  116.5 5.1 %copy-start.20 = (bf16[1,512,384]{1,2,0:T(8,128)(2,1)S(1)}, bf16[1,512,384]{1,2,0:T(8,128)(2,1)}, u32[]{:S(2)}) copy-start(bf16[1,512,384]{1,2,0:T(8,128)(2,1)} %copy-done.19) | copy-start | bytes 1179652
  127.2 3.1 %copy-start.22 = (bf16[512,6,32]{0,2,1:T(8,128)(2,1)S(1)}, bf16[512,6,32]{0,2,1:T(8,128)(2,1)}, u32[]{:S(2)}) copy-start(bf16[512,6,32]{0,2,1:T(8,128)(2,1)} %copy-done.21) | copy-start | bytes 589828
  130.3 3.5 %copy-start.37 = (f32[512,32]{0,1:T(8,128)S(1)}, f32[512,32]{0,1:T(8,128)}, u32[]{:S(2)}) copy-start(f32[512,32]{0,1:T(8,128)} %get-tuple-element.57) | copy-start | bytes 196612
  137.1 4.9 %copy-start.16 = (bf16[512,768]{1,0:T(8,128)(2,1)S(1)}, bf16[512,768]{1,0:T(8,128)(2,1)}, u32[]{:S(2)}) copy-start(bf16[512,768]{1,0:T(8,128)(2,1)} %copy-done.15) | copy-start | bytes 2359300
  137.1 4.9 %copy-start.31 = (bf16[512,576]{0,1:T(8,128)(2,1)S(1)}, bf16[512,576]{0,1:T(8,128)(2,1)}, u32[]{:S(2)}) copy-start(bf16[512,576]{0,1:T(8,128)(2,1)} %get-tuple-element.35) | copy-start | bytes 1769476
  141.1 87.3 %reduce-scatter.7.cloned.1.call-start = ((), (), s32[]{:S(2)}) async-start(), calls=%async_computation.5 | async-start | bytes 1179648 | tf_op jit(solution)/shard_map/reduce_scatter | solution.py:261
  153.3 3.1 %copy-start.28 = (bf16[512,768]{1,0:T(8,128)(2,1)S(1)}, bf16[512,768]{1,0:T(8,128)(2,1)}, u32[]{:S(2)}) copy-start(bf16[512,768]{1,0:T(8,128)(2,1)} %copy-done.27) | copy-start | bytes 2359300
  165.9 3.8 %copy-start.45 = (f32[1,768]{1,0:T(1,128)S(1)}, f32[1,768]{1,0:T(1,128)}, u32[]{:S(2)}) copy-start(f32[1,768]{1,0:T(1,128)} %broadcast_in_dim.42) | copy-start | bytes 9220
  165.9 3.8 %copy-start.48 = (f32[8]{0:T(128)S(1)}, f32[8]{0:T(128)}, u32[]{:S(2)}) copy-start(f32[8]{0:T(128)} %pad.7.clone) | copy-start | bytes 100
  (32 other events, 50.9 us)
Sparse Core Ops, SparseCore 0:
  37.9 20.3 reduce-scatter.4
  82.0 18.6 reduce-scatter.8
  141.2 17.4 reduce-scatter.10
  160.9 17.4 reduce-scatter.6
